TPU v7x, 32 devices: a whole 2x2x4 slice. The times are simulated.
32 devices in a mesh: groups: 2 (over y), expert: 4 (over z), tensor: 4 (over x, core).
Axes of the slice: x: 2, y: 2, z: 4, core: 2. Of those that a mesh axis runs over, the one named last changes fastest.
Arguments:
- mixer_input: bfloat16 [64, 512], P('groups', ('expert', 'tensor')), parts along dimension 0, may hold values from -6 to 6
- mixer_gate: bfloat16 [64, 512], P('groups', ('expert', 'tensor')), parts along dimension 0, may hold values from -6 to 6
- conv_state: bfloat16 [16, 3, 512], P('groups', None, ('expert', 'tensor')), parts along dimension 0, may hold values from -6 to 6
- conv_weight: float32 [4, 512], P(None, ('expert', 'tensor')), may hold values from -3 to 3
- conv_bias: float32 [512], P(('expert', 'tensor')), may hold values from -3 to 3
- ssm_state: float32 [16, 16, 512], P('groups', None, ('expert', 'tensor')), parts along dimension 0, may hold values from -6 to 6
- decay_rate: float32 [16, 512], P(None, ('expert', 'tensor')), may hold values from 0.01 to 2
- step_bias: float32 [512], P(('expert', 'tensor')), may hold values from -4 to -1
- skip_gain: float32 [512], P(('expert', 'tensor')), may hold values from 0.5 to 1.5
- state_proj: bfloat16 [512, 288], P(('expert', 'tensor')), may hold values from -0.25 to 0.25
- step_proj: bfloat16 [256, 512], P(None, ('expert', 'tensor')), may hold values from -0.375 to 0.375
- out_proj: bfloat16 [512, 4096], P('expert', 'tensor'), may hold values from -0.25 to 0.25
- residual: bfloat16 [64, 4096], P(('groups', 'expert'), 'tensor'), parts along dimension 0, may hold values from -6 to 6
- norm_gain: float32 [4096], P('tensor'), may hold values from 0.5 to 1.5
- expert_gate: bfloat16 [4096, 32768], P(None, ('expert', 'tensor')), may hold values from -0.09375 to 0.09375
- expert_up: bfloat16 [4096, 32768], P(None, ('expert', 'tensor')), may hold values from -0.09375 to 0.09375
- expert_down: bfloat16 [32768, 4096], P(('expert', 'tensor')), may hold values from -0.046875 to 0.046875
- expert_ids: int32 [64, 2], P(('groups', 'expert')), parts along dimension 0, may hold values from 0 to 15, as said below
- route_gates: float32 [64, 2], P(('groups', 'expert')), parts along dimension 0, may hold values from 0.1 to 1
- request_lengths: int32 [16], P('groups'), parts along dimension 0, may hold values from 1 to 8, 32 in all
Outputs:
- layer_out: bfloat16 [64, 4096], P(('groups', 'expert'), 'tensor'), parts along dimension 0
- final_state: float32 [16, 16, 512], P('groups', None, ('expert', 'tensor')), parts along dimension 0
There are 2 independent parts, one for each index of `groups`. A program takes and returns all parts, laid end to end along the dimension named above; an argument that names none is the same for every part. Nothing has to cross between parts.
Inputs may be any that keep to these rules, and one draw needn't show every extreme that they name: `expert_ids`: each row names two different experts. Within each aligned block of 8 rows, each expert below 2 is named by at least one and at most 2 rows; one of them is named by exactly 2 rows in every block.
All inputs are finite; a program needn't handle non-finite values.
Results may differ from a plain program's by a relative error of at most 0.0057.
Values may be sent and summed in bfloat16 or wider, within the bound.
A program may use at most 128 MiB of HBM per device.

v0:
```python
import jax
import jax.numpy as jnp
from jax import lax
from jax.sharding import PartitionSpec as P

D = 4096
EXP_WIN = 2
CAP = 2


EPSILON = 1e-05


def convolve(mixer_input, conv_state, conv_weight, conv_bias, request_lengths):
    total_rows = mixer_input.shape[0]
    request_ends = jnp.cumsum(request_lengths)
    request_starts = request_ends - request_lengths
    places = jnp.arange(total_rows, dtype=jnp.int32)
    request = jnp.sum((places[:, None] >= request_ends[None, :]).astype(jnp.int32), axis=1)
    first_pos = jnp.take(request_starts, request)
    kernel_width = conv_weight.shape[0]
    summed = jnp.zeros(mixer_input.shape, jnp.float32) + conv_bias[None, :]
    for tap_index in range(kernel_width):
        shift_back = kernel_width - 1 - tap_index
        source = places - shift_back
        inside = source >= first_pos
        from_span = jnp.take(mixer_input, jnp.maximum(source, 0), axis=0).astype(jnp.float32)
        state_slot = jnp.clip(source - first_pos + kernel_width - 1, 0, kernel_width - 2)
        from_state = conv_state[request, state_slot].astype(jnp.float32)
        summed = summed + conv_weight[tap_index][None, :] * jnp.where(
            inside[:, None], from_span, from_state
        )
    return (jax.nn.silu(summed).astype(jnp.bfloat16), request, first_pos, request_ends)


def select_scan(
    conv_float,
    step_size,
    input_map,
    output_map,
    decay_rate,
    ssm_state,
    request,
    first_pos,
    request_ends,
):
    token_count = conv_float.shape[0]
    state_count = decay_rate.shape[0]
    channel_count = decay_rate.shape[1]
    flat_width = state_count * channel_count
    places = jnp.arange(token_count, dtype=jnp.int32)
    opening = (places == first_pos)[:, None]
    step_tiled = jnp.tile(step_size, (1, state_count))
    decay_now = jnp.exp(-step_tiled * decay_rate.reshape(1, flat_width))
    driven = jnp.tile(step_size * conv_float, (1, state_count)) * jnp.repeat(
        input_map, channel_count, axis=1
    )
    initial = jnp.take(ssm_state.reshape(ssm_state.shape[0], flat_width), request, axis=0)
    driven = jnp.where(opening, decay_now * initial + driven, driven)
    decay_now = jnp.where(opening, 0.0, decay_now)

    def combine(earlier, later_one):
        return (earlier[0] * later_one[0], later_one[0] * earlier[1] + later_one[1])

    carried = lax.associative_scan(combine, (decay_now, driven), axis=0)[1]
    weighted = carried * jnp.repeat(output_map, channel_count, axis=1)
    scanned = jnp.sum(weighted.reshape(token_count, state_count, channel_count), axis=1)
    final_state = jnp.take(carried, request_ends - 1, axis=0).reshape(ssm_state.shape)
    return (scanned, final_state)


def body(
    mixer_input,
    mixer_gate,
    conv_state,
    conv_weight,
    conv_bias,
    ssm_state,
    decay_rate,
    step_bias,
    skip_gain,
    state_proj,
    step_proj,
    out_proj,
    residual,
    norm_gain,
    expert_gate,
    expert_up,
    expert_down,
    expert_ids,
    route_gates,
    request_lengths,
):
    conv_out, request, first_pos, request_ends = convolve(
        mixer_input, conv_state, conv_weight, conv_bias, request_lengths
    )
    partial_proj = jnp.dot(conv_out, state_proj, preferred_element_type=jnp.float32)
    projected = lax.psum(partial_proj, ("expert", "tensor"))
    rank_width = step_proj.shape[0]
    state_count = decay_rate.shape[0]
    step_low = projected[:, :rank_width].astype(jnp.bfloat16)
    input_map = projected[:, rank_width : rank_width + state_count]
    output_map = projected[:, rank_width + state_count :]
    step_size = jax.nn.softplus(
        jnp.dot(step_low, step_proj, preferred_element_type=jnp.float32) + step_bias[None, :]
    )
    conv_float = conv_out.astype(jnp.float32)
    scanned, final_state = select_scan(
        conv_float,
        step_size,
        input_map,
        output_map,
        decay_rate,
        ssm_state,
        request,
        first_pos,
        request_ends,
    )
    mixed_out = (
        (scanned + skip_gain[None, :] * conv_float) * jax.nn.silu(mixer_gate.astype(jnp.float32))
    ).astype(jnp.bfloat16)
    mixer_part = jnp.dot(
        lax.all_gather(mixed_out, "tensor", axis=1, tiled=True),
        out_proj,
        preferred_element_type=jnp.float32,
    )
    mixer_sum = lax.psum_scatter(mixer_part, "expert", scatter_dimension=0, tiled=True)
    stream = residual.astype(jnp.float32) + mixer_sum
    squares = lax.psum(jnp.sum(stream * stream, axis=1), "tensor")
    normed = (stream * lax.rsqrt(squares / D + EPSILON)[:, None] * norm_gain[None, :]).astype(
        jnp.bfloat16
    )
    expert_count = lax.axis_size("expert")
    group_size = expert_count // EXP_WIN
    labels = jnp.arange(EXP_WIN, dtype=jnp.int32)
    named_here = expert_ids[:, :, None] == labels[None, None, :]
    member = jnp.any(named_here, axis=1).astype(jnp.int32)
    weights_row = jnp.sum(jnp.where(named_here, route_gates[:, :, None], 0.0), axis=1)
    placed = jnp.cumsum(member, axis=0) - 1
    slot_ids = jnp.arange(CAP, dtype=jnp.int32)
    chosen = (member[:, :, None] == 1) & (placed[:, :, None] == slot_ids[None, None, :])
    select = chosen.astype(jnp.bfloat16)
    owners = jnp.arange(expert_count, dtype=jnp.int32) // group_size
    routed = jnp.take(select, owners, axis=1)
    outgoing = jnp.einsum("rnc,rd->ncd", routed, normed, preferred_element_type=jnp.float32).astype(
        jnp.bfloat16
    )
    arrived = lax.all_to_all(outgoing, "expert", split_axis=0, concat_axis=0, tiled=True)
    arrived = arrived.reshape(-1, arrived.shape[2])
    shard_piece = lax.all_gather(arrived, "tensor", axis=1, tiled=True)
    gate_acc = jnp.dot(shard_piece, expert_gate, preferred_element_type=jnp.float32)
    up_acc = jnp.dot(shard_piece, expert_up, preferred_element_type=jnp.float32)
    hidden_act = (jax.nn.silu(gate_acc) * up_acc).astype(jnp.bfloat16)
    partial_out = jnp.dot(hidden_act, expert_down, preferred_element_type=jnp.float32)
    returned = lax.all_to_all(
        partial_out.reshape(expert_count, CAP, partial_out.shape[1]).astype(jnp.bfloat16),
        "expert",
        split_axis=0,
        concat_axis=0,
        tiled=True,
    ).astype(jnp.float32)
    grouped = jnp.sum(returned.reshape(EXP_WIN, group_size, CAP, returned.shape[2]), axis=1)
    values = lax.psum_scatter(grouped, "tensor", scatter_dimension=2, tiled=True)
    scaled = select.astype(jnp.float32) * weights_row[:, :, None]
    expert_sum = jnp.einsum("rwc,wcd->rd", scaled, values, precision=lax.Precision.HIGHEST)
    layer_out = (stream + expert_sum).astype(jnp.bfloat16)
    return (layer_out, final_state)


def solution(mesh):
    in_specs = (
        P("groups", ("expert", "tensor")),
        P("groups", ("expert", "tensor")),
        P("groups", None, ("expert", "tensor")),
        P(None, ("expert", "tensor")),
        P(("expert", "tensor")),
        P("groups", None, ("expert", "tensor")),
        P(None, ("expert", "tensor")),
        P(("expert", "tensor")),
        P(("expert", "tensor")),
        P(("expert", "tensor"), None),
        P(None, ("expert", "tensor")),
        P("expert", "tensor"),
        P(("groups", "expert"), "tensor"),
        P("tensor"),
        P(None, ("expert", "tensor")),
        P(None, ("expert", "tensor")),
        P(("expert", "tensor"), None),
        P(("groups", "expert"), None),
        P(("groups", "expert"), None),
        P("groups"),
    )
    out_specs = (P(("groups", "expert"), "tensor"), P("groups", None, ("expert", "tensor")))
    return jax.shard_map(body, mesh=mesh, in_specs=in_specs, out_specs=out_specs, check_vma=False)
```

profile of v0, /device:TPU:0, one launch (start us, length us, event | category | flops | bytes accessed | tf_op | source)
XLA Modules:
  0.0 217.6 jit_solution(16373003492878667524)
XLA Ops:
  7.2 0.0 copy-start
  7.2 0.0 reduce-scatter.5.cloned.1.call-start
  7.2 0.9 reduce-window.4
  8.1 0.7 bitcast_subtract_fusion
  8.7 0.1 convert_reduce_fusion.1
  8.8 0.7 gather_fusion
  9.7 1.4 gather_fusion.2
  11.1 1.4 gather_fusion.3
  12.4 1.4 gather_fusion.4
  13.8 1.4 gather_fusion.1
  15.2 0.8 slice_bitcast_fusion.3
  16.0 1.3 gather_fusion.8
  17.3 1.3 gather_fusion.9
  18.6 1.3 gather_fusion.10
  19.9 1.3 gather_fusion.11
  21.2 0.8 multiply_convert_fusion.1
  21.9 0.9 fusion.66
  22.8 63.0 %psum.14 = f32[32,288]{1,0:T(8,128)S(1)} all-reduce(f32[32,288]{1,0:T(8,128)S(1)} %fusion.66), channel_id=1, replica_groups=mesh['groups'=2,'expert'=4,'tensor'=4] {'expert','tensor'}, use_global_device_ids=true, to_apply=%region_2.4 | all-reduce | flops 9216 | bytes 73728 | tf_op jit(solution)/shard_map/psum | solution.py:98
  85.8 0.1 fusion.59
  85.9 0.9 fusion.62
  86.8 0.1 broadcast_multiply_fusion
  86.9 0.1 mul.175
  87.1 0.1 neg.25
  87.2 0.9 reshape.344
  88.1 0.6 gather_fusion.5
  88.7 0.8 mul.169
  89.5 0.1 fusion.8
  90.5 0.1 broadcast_in_dim.144
  90.6 0.1 reshape.345
  90.8 0.1 reshape.346
  91.0 0.7 fusion.13
  91.7 0.1 copy.36
  91.8 5.2 %all_gather.6 = bf16[32,128]{0,1:T(8,128)(2,1)S(1)} all-gather(bf16[32,32]{0,1:T(8,128)(2,1)S(1)} %copy.36), channel_id=1, replica_groups=mesh['groups'=2,'expert'=4,'tensor'=4] {'tensor'}, dimensions={1}, use_global_device_ids=true | all-gather | bytes 10240 | tf_op jit(solution)/shard_map/all_gather | solution.py:123
  97.0 0.8 fusion.67
  97.8 0.0 reduce-scatter.5.cloned.1.call-update
  97.9 0.7 fusion.29
  98.6 0.2 reduce_window_sum.18
  98.8 0.6 gather_fusion.6
  99.4 0.1 fusion.30
  99.5 15.1 %reduce-scatter.5.cloned.1.call-done = f32[8,1024]{1,0:T(8,128)} async-done(((f32[32,1024]{1,0:T(8,128)}), f32[8,1024]{1,0:T(8,128)}) %reduce-scatter.5.cloned.1.call-update) | async-done | bytes 32784 | tf_op jit(solution)/shard_map/reduce_scatter | solution.py:127
  114.5 0.9 multiply_reduce_fusion
  115.4 5.7 %psum.15 = f32[8]{0:T(128)S(1)} all-reduce(f32[8]{0:T(128)S(1)} %multiply_reduce_fusion), channel_id=1, replica_groups=mesh['groups'=2,'expert'=4,'tensor'=4] {'tensor'}, use_global_device_ids=true, to_apply=%region_9.11 | all-reduce | flops 8 | bytes 64 | tf_op jit(solution)/shard_map/psum | solution.py:129
  121.1 1.0 convolution_convert_fusion.1
  122.0 0.6 copy.38
  122.7 3.3 %all-to-all-start = ((bf16[4,2,1024]{2,1,0:T(2,128)(2,1)}), bf16[4,2,1024]{2,1,0:T(2,128)(2,1)S(1)}, u32[]{:S(2)}, u32[]{:S(2)}) async-start(bf16[4,2,1024]{2,1,0:T(2,128)(2,1)} %copy.38), calls=%async_computation.1 | async-start | bytes 32768 | tf_op jit(solution)/shard_map/all_to_all | solution.py:148
  125.9 5.6 %all-to-all-done = bf16[4,2,1024]{2,1,0:T(2,128)(2,1)S(1)} async-done(((bf16[4,2,1024]{2,1,0:T(2,128)(2,1)}), bf16[4,2,1024]{2,1,0:T(2,128)(2,1)S(1)}, u32[]{:S(2)}, u32[]{:S(2)}) %all-to-all-start) | async-done | bytes 16416 | tf_op jit(solution)/shard_map/all_to_all | solution.py:148
  131.5 5.2 %all_gather.7 = bf16[8,4096]{1,0:T(8,128)(2,1)S(1)} all-gather(bf16[8,1024]{1,0:T(8,128)(2,1)S(1)} %reshape.347), channel_id=1, replica_groups=mesh['groups'=2,'expert'=4,'tensor'=4] {'tensor'}, dimensions={1}, use_global_device_ids=true | all-gather | bytes 81920 | tf_op jit(solution)/shard_map/all_gather | solution.py:150
  136.8 8.0 %fusion.68 = f32[8,2048]{1,0:T(8,128)S(1)} fusion(bf16[8,4096]{1,0:T(8,128)(2,1)S(1)} %all_gather.7, bf16[4096,2048]{1,0:T(8,128)(2,1)} %param.36), kind=kOutput, calls=%fused_computation.171 | convolution fusion | flops 134217728 | bytes 16908288 | tf_op jit(solution)/shard_map/dot_general | solution.py:151
  144.8 12.9 %convolution_convert_fusion = bf16[8,4096]{1,0:T(8,128)(2,1)S(1)} fusion(bf16[2048,4096]{1,0:T(8,128)(2,1)} %param.38, bf16[8,4096]{1,0:T(8,128)(2,1)S(1)} %all_gather.7, bf16[4096,2048]{1,0:T(8,128)(2,1)} %param.37, f32[8,2048]{1,0:T(8,128)S(1)} %fusion.68), kind=kOutput, calls=%fused_computation.12 | convolution fusion | flops 268566528 | bytes 33751040 | tf_op jit(solution)/shard_map/dot_general | solution.py:154
  157.7 0.7 convert_element_type.100
  158.4 3.3 %all-to-all-start.1 = ((bf16[4,2,4096]{2,1,0:T(2,128)(2,1)}), bf16[4,2,4096]{2,1,0:T(2,128)(2,1)S(1)}, u32[]{:S(2)}, u32[]{:S(2)}) async-start(bf16[4,2,4096]{2,1,0:T(2,128)(2,1)} %convert_element_type.100), calls=%async_computation.2 | async-start | bytes 131072 | tf_op jit(solution)/shard_map/all_to_all | solution.py:155
  161.7 0.2 reduce-scatter.7.cloned.1.call-start
  161.9 0.6 gather_fusion.7
  162.5 0.1 gather.44
  162.6 4.8 %all-to-all-done.1 = bf16[4,2,4096]{2,1,0:T(2,128)(2,1)S(1)} async-done(((bf16[4,2,4096]{2,1,0:T(2,128)(2,1)}), bf16[4,2,4096]{2,1,0:T(2,128)(2,1)S(1)}, u32[]{:S(2)}, u32[]{:S(2)}) %all-to-all-start.1) | async-done | bytes 65568 | tf_op jit(solution)/shard_map/all_to_all | solution.py:155
  167.4 0.1 convert_reduce_fusion
  167.5 4.4 %copy.41 = f32[2,2,4096]{0,1,2:T(2,128)} copy(f32[2,2,4096]{2,1,0:T(2,128)S(1)} %convert_reduce_fusion) | data formatting | bytes 131072
  171.8 5.4 %reshape.454 = f32[4096,4]{1,0:T(8,128)} reshape(f32[4096,2,2]{2,1,0:T(2,128)} %bitcast.74) | data formatting | bytes 131072
  177.3 0.0 reduce-scatter.7.cloned.1.call-update
  177.3 0.7 broadcast_select_fusion
  178.0 29.8 %reduce-scatter.7.cloned.1.call-done = f32[1024,4]{1,0:T(8,128)} async-done(((f32[4096,4]{1,0:T(8,128)}), f32[1024,4]{1,0:T(8,128)}) %reduce-scatter.7.cloned.1.call-update) | async-done | bytes 16400
  207.8 1.6 reshape.455
  209.5 0.5 copy.40
  209.9 0.9 fusion.2
  (90 shorter events, 1.0 us)
Async XLA Ops:
  7.2 89.8 %copy-start = (bf16[128,1024]{1,0:T(8,128)(2,1)S(1)}, bf16[128,1024]{1,0:T(8,128)(2,1)}, u32[]{:S(2)}) copy-start(bf16[128,1024]{1,0:T(8,128)(2,1)} %param.33) | copy-start | bytes 786436
  7.2 107.3 %reduce-scatter.5.cloned.1.call-start = ((), (), s32[]{:S(2)}) async-start(), calls=%async_computation.4 | async-start | bytes 163840 | tf_op jit(solution)/shard_map/reduce_scatter | solution.py:127
  122.7 8.8 %all-to-all-start = ((bf16[4,2,1024]{2,1,0:T(2,128)(2,1)}), bf16[4,2,1024]{2,1,0:T(2,128)(2,1)S(1)}, u32[]{:S(2)}, u32[]{:S(2)}) async-start(bf16[4,2,1024]{2,1,0:T(2,128)(2,1)} %copy.38), calls=%async_computation.1 | async-start | bytes 32768 | tf_op jit(solution)/shard_map/all_to_all | solution.py:148
  144.8 33.2 %copy-start.3 = (s32[8,2]{0,1:T(2,128)S(1)}, s32[8,2]{0,1:T(2,128)}, u32[]{:S(2)}) copy-start(s32[8,2]{0,1:T(2,128)} %param.39) | copy-start | bytes 196
  144.8 33.2 %copy-start.4 = (f32[8,2]{0,1:T(2,128)S(1)}, f32[8,2]{0,1:T(2,128)}, u32[]{:S(2)}) copy-start(f32[8,2]{0,1:T(2,128)} %param.40) | copy-start | bytes 196
  144.8 65.1 %copy-start.1 = (f32[8,1024]{1,0:T(8,128)S(1)}, f32[8,1024]{1,0:T(8,128)}, u32[]{:S(2)}) copy-start(f32[8,1024]{1,0:T(8,128)} %reduce-scatter.5.cloned.1.call-done) | copy-start | bytes 98308
  144.8 65.1 %copy-start.2 = (bf16[8,1024]{1,0:T(8,128)(2,1)S(1)}, bf16[8,1024]{1,0:T(8,128)(2,1)}, u32[]{:S(2)}) copy-start(bf16[8,1024]{1,0:T(8,128)(2,1)} %param.34) | copy-start | bytes 49156
  158.4 9.0 %all-to-all-start.1 = ((bf16[4,2,4096]{2,1,0:T(2,128)(2,1)}), bf16[4,2,4096]{2,1,0:T(2,128)(2,1)S(1)}, u32[]{:S(2)}, u32[]{:S(2)}) async-start(bf16[4,2,4096]{2,1,0:T(2,128)(2,1)} %convert_element_type.100), calls=%async_computation.2 | async-start | bytes 131072 | tf_op jit(solution)/shard_map/all_to_all | solution.py:155
  161.7 46.1 %reduce-scatter.7.cloned.1.call-start = ((), (), s32[]{:S(2)}) async-start(), calls=%async_computation.5 | async-start | bytes 2621440
Sparse Core Ops, SparseCore 0:
  98.0 16.4 reduce-scatter.4
  177.4 30.3 reduce-scatter.6
where the time goes:
time: 219 us; the launch traced here: 218 us
  blocking collectives  79.1 us (36%)
  waiting for transfers between devices  55.3 us (25%)
  local copies, waits for them, and re-layouts  30.3 us (14%)
  matrix products  25.3 us (12%)
  between operations  14.5 us (7%)
  starting transfers between devices  6.8 us (3%)
  other arithmetic  6.36 us (3%)
    psum x1, blocking collectives, body(): projected = lax.psum(partial_proj, ('expert', 'tensor'))  63 us
    unnamed x3, waiting for transfers between devices  29.8 us
    reduce_scatter x1, waiting for transfers between devices, body(): lax.psum_scatter(mixer_part, 'expert', scatter_dimension=0, tiled=True)  15.1 us
    dot_general x1, matrix products, body(): jnp.dot(hidden_act, expert_down, preferred_element_type=jnp.float32)  12.9 us
    unnamed x13, local copies, waits for them, and re-layouts  11.5 us
    dot_general x1, matrix products, body(): jnp.dot(shard_piece, expert_gate, preferred_element_type=jnp.float32)  8.03 us
    psum x1, blocking collectives, body(): squares = lax.psum(jnp.sum(stream * stream, axis=1), 'tensor')  5.67 us
    all_to_all x1, waiting for transfers between devices, body(): lax.all_to_all(outgoing, 'expert', split_axis=0, concat_axis=0, tiled=True)  5.56 us
  transfers between devices with their start and end apart: 4, of which 4 were waited for; matrix products, arithmetic and copies ran while one was open for 1% of the time, Pallas kernels for 0%

commit v1 on v0

v1 whole, which is shorter than its diff:
```python
import functools

import jax
import jax.numpy as jnp
from jax import lax
from jax.experimental import pallas as pl
from jax.experimental.pallas import tpu as pltpu
from jax.sharding import PartitionSpec as P

EXP_WIN = 2
CAP = 2
EPSILON = 1e-05
LANES = 128
MESH = pl.DeviceIdType.MESH
F32 = jnp.float32
BF16 = jnp.bfloat16


def silu(u):
    return u / (1.0 + jnp.exp(-u))


def kernel(
    n_expert,
    n_tensor,
    lengths_ref,
    ids_ref,
    gates_ref,
    mixer_input,
    mixer_gate,
    conv_state,
    conv_weight,
    conv_bias,
    ssm_state,
    decay_rate,
    step_bias,
    skip_gain,
    state_proj,
    step_proj,
    out_proj,
    residual,
    norm_gain,
    gate_hbm,
    up_hbm,
    down_hbm,
    layer_out,
    final_state,
    gate_v,
    up_v,
    down_v,
    shifted,
    part_send,
    part_recv,
    proj_send,
    proj_recv,
    proj_all,
    decay_all,
    drive_all,
    carried,
    mixed_all,
    mix_send,
    mix_recv,
    stream_s,
    tok_send,
    tok_recv,
    tokens_s,
    hidden,
    out_send,
    out_recv,
    load_sem,
    s1,
    r1,
    s2,
    r2,
    s3,
    r3,
    s4,
    r4,
    s5,
    r5,
    s6,
    r6,
):
    n_all = n_expert * n_tensor
    my_e = lax.axis_index("expert")
    my_t = lax.axis_index("tensor")
    me = my_e * n_tensor + my_t
    total, chans = mixer_input.shape
    requests = conv_state.shape[0]
    taps = conv_weight.shape[0]
    states = decay_rate.shape[0]
    rank = step_proj.shape[0]
    rows_each = total // n_all
    toks, feats = residual.shape
    width = feats * n_tensor
    group = n_expert // EXP_WIN
    held = n_expert * CAP

    loads = [
        pltpu.make_async_copy(src, dst, load_sem.at[i])
        for i, (src, dst) in enumerate(((gate_hbm, gate_v), (up_hbm, up_v), (down_hbm, down_v)))
    ]
    for load in loads:
        load.start()

    def other(k):
        d = lax.rem(me + k, n_all)
        return d, d // n_tensor, lax.rem(d, n_tensor)

    def at(e, t):
        return {"expert": e, "tensor": t}

    barrier = pltpu.get_barrier_semaphore()

    def greet(k, _):
        d, e, t = other(k)
        pl.semaphore_signal(barrier, inc=1, device_id=at(e, t), device_id_type=MESH)
        return 0

    lax.fori_loop(1, n_all, greet, 0)

    starts, ends = [], []
    run = jnp.int32(0)
    for r in range(requests):
        starts.append(run)
        run = run + lengths_ref[r]
        ends.append(run)
    place = lax.broadcasted_iota(jnp.int32, (total, chans), 0)
    first = jnp.zeros((total, chans), jnp.int32)
    from_state = [jnp.zeros((total, chans), F32) for _ in range(taps - 1)]
    for r in range(requests):
        inside = place >= starts[r]
        first = jnp.where(inside, starts[r], first)
        old = conv_state[r].astype(F32)
        for j in range(taps - 1):
            from_state[j] = jnp.where(inside, old[j : j + 1, :], from_state[j])
    since = place - first
    shifted[0:8, :] = jnp.zeros((8, chans), F32)
    shifted[8:, :] = mixer_input[...].astype(F32)
    summed = jnp.zeros((total, chans), F32) + conv_bias[...]
    for k in range(taps):
        back = taps - 1 - k
        value = shifted[8 - back : 8 - back + total, :]
        if back:
            carried_in = from_state[0]
            for j in range(1, taps - 1):
                carried_in = jnp.where(since - back + taps - 1 == j, from_state[j], carried_in)
            value = jnp.where(since >= back, value, carried_in)
        summed = summed + conv_weight[k : k + 1, :] * value
    conv_out = silu(summed).astype(BF16)
    conv_float = conv_out.astype(F32)

    partial = jnp.dot(conv_out, state_proj[...], preferred_element_type=F32)
    for d in range(n_all):
        part_send[d] = partial[d * rows_each : (d + 1) * rows_each, :]
    part_recv[me] = part_send[me]

    pl.semaphore_wait(barrier, n_all - 1)

    def copy1(k):
        d, e, t = other(k)
        return pltpu.make_async_remote_copy(
            src_ref=part_send.at[d],
            dst_ref=part_recv.at[me],
            send_sem=s1.at[k],
            recv_sem=r1.at[k],
            device_id=at(e, t),
            device_id_type=MESH,
        )

    def copy2(k):
        d, e, t = other(k)
        return pltpu.make_async_remote_copy(
            src_ref=proj_send,
            dst_ref=proj_recv.at[me],
            send_sem=s2.at[k],
            recv_sem=r2.at[k],
            device_id=at(e, t),
            device_id_type=MESH,
        )

    def start_all(copy, count):
        lax.fori_loop(1, count, lambda k, c: (copy(k).start(), c)[1], 0)

    def receive_all(copy, count):
        lax.fori_loop(1, count, lambda k, c: (copy(k).wait_recv(), c)[1], 0)

    def sent_all(copy, count):
        lax.fori_loop(1, count, lambda k, c: (copy(k).wait_send(), c)[1], 0)

    start_all(copy1, n_all)
    receive_all(copy1, n_all)
    proj_send[...] = jnp.sum(part_recv[...], axis=0)
    start_all(copy2, n_all)
    proj_recv[me] = proj_send[...]

    slots = []
    for w in range(EXP_WIN):
        count = jnp.int32(0)
        index = [jnp.int32(0) for _ in range(CAP)]
        weight = [jnp.float32(0) for _ in range(CAP)]
        for row in range(toks):
            zero = ids_ref[row, 0] == w
            one = ids_ref[row, 1] == w
            named = jnp.logical_or(zero, one)
            gate = jnp.where(zero, gates_ref[row, 0], 0.0) + jnp.where(one, gates_ref[row, 1], 0.0)
            for s in range(CAP):
                here = jnp.logical_and(named, count == s)
                index[s] = jnp.where(here, row, index[s])
                weight[s] = jnp.where(here, gate, weight[s])
            count = count + named.astype(jnp.int32)
        slots.append((index, weight))

    receive_all(copy2, n_all)
    for d in range(n_all):
        proj_all[d * rows_each : (d + 1) * rows_each, :] = proj_recv[d]
    projected = proj_all[...]
    step_low = projected[:, :rank].astype(BF16)
    input_map = projected[:, rank : rank + states]
    output_map = projected[:, rank + states :]
    raw = jnp.dot(step_low, step_proj[...], preferred_element_type=F32) + step_bias[...]
    step = jnp.maximum(raw, 0.0) + jnp.log1p(jnp.exp(-jnp.abs(raw)))

    decay_all[...] = jnp.exp(-step[:, None, :] * decay_rate[...][None, :, :])
    drive_all[...] = (step * conv_float)[:, None, :] * input_map[:, :, None]

    def advance(t, carry):
        h, r, begin, end = carry
        before = jnp.where(t == begin, ssm_state[r], h)
        h = decay_all[t] * before + drive_all[t]
        carried[t] = h
        over = t + 1 == end
        following = jnp.minimum(r + 1, requests - 1)
        return (
            h,
            jnp.where(over, following, r),
            jnp.where(over, end, begin),
            jnp.where(over, end + lengths_ref[following], end),
        )

    lax.fori_loop(
        0,
        total,
        advance,
        (jnp.zeros((states, chans), F32), jnp.int32(0), jnp.int32(0), ends[0]),
    )
    for r in range(requests):
        final_state[r] = carried[jnp.clip(ends[r] - 1, 0, total - 1)]
    scanned = jnp.sum(carried[...] * output_map[:, :, None], axis=1)
    mixed = (scanned + skip_gain[...] * conv_float) * silu(mixer_gate[...].astype(F32))
    mixed_all[my_t] = mixed.astype(BF16)

    def copy3(k):
        return pltpu.make_async_remote_copy(
            src_ref=mixed_all.at[my_t],
            dst_ref=mixed_all.at[my_t],
            send_sem=s3.at[k],
            recv_sem=r3.at[k],
            device_id=at(my_e, lax.rem(my_t + k, n_tensor)),
            device_id_type=MESH,
        )

    start_all(copy3, n_tensor)
    receive_all(copy3, n_tensor)
    part = jnp.zeros((total, feats), F32)
    for t in range(n_tensor):
        part = part + jnp.dot(
            mixed_all[t], out_proj[t * chans : (t + 1) * chans, :], preferred_element_type=F32
        )
    half = feats // 2
    for e in range(n_expert):
        rows = part[e * toks : (e + 1) * toks, :]
        mix_send[e] = jnp.concatenate([rows[:, :half], rows[:, half:]], axis=0).astype(BF16)
    mix_recv[my_e] = mix_send[my_e]

    def copy4(k):
        e = lax.rem(my_e + k, n_expert)
        return pltpu.make_async_remote_copy(
            src_ref=mix_send.at[e],
            dst_ref=mix_recv.at[my_e],
            send_sem=s4.at[k],
            recv_sem=r4.at[k],
            device_id=at(e, my_t),
            device_id_type=MESH,
        )

    start_all(copy4, n_expert)
    receive_all(copy4, n_expert)
    mix = jnp.sum(mix_recv[...].astype(F32), axis=0)
    stream = residual[...].astype(F32) + jnp.concatenate([mix[:toks], mix[toks:]], axis=1)
    squares = jnp.sum(stream * stream, axis=1, keepdims=True)
    stream_s[:, :feats] = stream * norm_gain[...]
    stream_s[:, feats:] = jnp.broadcast_to(squares, (toks, LANES))

    for w in range(EXP_WIN):
        for s in range(CAP):
            tok_send[w, s : s + 1, :] = stream_s[pl.ds(slots[w][0][s], 1), :]
    tok_recv[me] = tok_send[my_e // group]

    def copy5(k):
        d, e, t = other(k)
        return pltpu.make_async_remote_copy(
            src_ref=tok_send.at[e // group],
            dst_ref=tok_recv.at[me],
            send_sem=s5.at[k],
            recv_sem=r5.at[k],
            device_id=at(e, t),
            device_id_type=MESH,
        )

    start_all(copy5, n_all)
    receive_all(copy5, n_all)
    padded = tokens_s.shape[0]
    if padded > held:
        tokens_s[held:, :] = jnp.zeros((padded - held, width + LANES), F32)
    for e in range(n_expert):
        square = jnp.zeros((CAP, LANES), F32)
        for t in range(n_tensor):
            got = tok_recv[e * n_tensor + t]
            tokens_s[e * CAP : (e + 1) * CAP, t * feats : (t + 1) * feats] = got[:, :feats]
            square = square + got[:, feats:]
        tokens_s[e * CAP : (e + 1) * CAP, width:] = square
    scale = lax.rsqrt(tokens_s[:, width : width + 1] / width + EPSILON)
    normed = (tokens_s[:, :width] * scale).astype(BF16)

    loads[0].wait()
    loads[1].wait()
    units = gate_v.shape[1]
    tile = 256 if units % 256 == 0 else units

    def unit_tile(i, c):
        cols = pl.ds(pl.multiple_of(i * tile, tile), tile) if units > tile else slice(None)
        g = jnp.dot(normed, gate_v[:, cols], preferred_element_type=F32)
        u = jnp.dot(normed, up_v[:, cols], preferred_element_type=F32)
        hidden[:, cols] = (silu(g) * u).astype(BF16)
        return c

    lax.fori_loop(0, units // tile, unit_tile, 0)
    loads[2].wait()
    act = hidden[...]
    otile = 512 if feats % 512 == 0 else feats

    def out_tile(i, c):
        cols = pl.ds(pl.multiple_of(i * otile, otile), otile)
        got = jnp.dot(act, down_v[:, cols], preferred_element_type=F32)
        for e in range(n_expert):
            out_send[e, :, cols] = got[e * CAP : (e + 1) * CAP, :]
        return c

    def copy6(k):
        d, e, t = other(k)
        return pltpu.make_async_remote_copy(
            src_ref=out_send.at[e, :, pl.ds(pl.multiple_of(t * feats, LANES), feats)],
            dst_ref=out_recv.at[me],
            send_sem=s6.at[k],
            recv_sem=r6.at[k],
            device_id=at(e, t),
            device_id_type=MESH,
        )

    lax.fori_loop(0, width // otile, out_tile, 0)
    start_all(copy6, n_all)
    out_recv[me] = out_send[my_e, :, pl.ds(pl.multiple_of(my_t * feats, LANES), feats)]
    receive_all(copy6, n_all)
    row_id = lax.broadcasted_iota(jnp.int32, (toks, feats), 0)
    result = residual[...].astype(F32) + jnp.concatenate([mix[:toks], mix[toks:]], axis=1)
    share = group * n_tensor
    for w in range(EXP_WIN):
        value = jnp.sum(out_recv[w * share : (w + 1) * share], axis=0)
        for s in range(CAP):
            index, weight = slots[w]
            result = result + jnp.where(row_id == index[s], weight[s], 0.0) * value[s : s + 1, :]
    layer_out[...] = result.astype(BF16)
    for copy, count in (
        (copy1, n_all),
        (copy2, n_all),
        (copy3, n_tensor),
        (copy4, n_expert),
        (copy5, n_all),
        (copy6, n_all),
    ):
        sent_all(copy, count)


def body(
    n_expert,
    n_tensor,
    mixer_input,
    mixer_gate,
    conv_state,
    conv_weight,
    conv_bias,
    ssm_state,
    decay_rate,
    step_bias,
    skip_gain,
    state_proj,
    step_proj,
    out_proj,
    residual,
    norm_gain,
    expert_gate,
    expert_up,
    expert_down,
    expert_ids,
    route_gates,
    request_lengths,
):
    n_all = n_expert * n_tensor
    total, chans = mixer_input.shape
    states = decay_rate.shape[0]
    xw = state_proj.shape[1]
    toks, feats = residual.shape
    width = feats * n_tensor
    rows_each = total // n_all
    held = -(-n_expert * CAP // 16) * 16
    smem = pl.BlockSpec(memory_space=pltpu.SMEM)
    vmem = pl.BlockSpec(memory_space=pltpu.VMEM)
    hbm = pl.BlockSpec(memory_space=pl.ANY)
    sem = pltpu.SemaphoreType.DMA
    return pl.pallas_call(
        functools.partial(kernel, n_expert, n_tensor),
        out_shape=(
            jax.ShapeDtypeStruct((toks, feats), BF16),
            jax.ShapeDtypeStruct(ssm_state.shape, F32),
        ),
        in_specs=[smem] * 3 + [vmem] * 14 + [hbm] * 3,
        out_specs=(vmem, vmem),
        scratch_shapes=[
            pltpu.VMEM(expert_gate.shape, BF16),
            pltpu.VMEM(expert_up.shape, BF16),
            pltpu.VMEM(expert_down.shape, BF16),
            pltpu.VMEM((total + 8, chans), F32),
            pltpu.VMEM((n_all, rows_each, xw), F32),
            pltpu.VMEM((n_all, rows_each, xw), F32),
            pltpu.VMEM((rows_each, xw), F32),
            pltpu.VMEM((n_all, rows_each, xw), F32),
            pltpu.VMEM((total, xw), F32),
            pltpu.VMEM((total, states, chans), F32),
            pltpu.VMEM((total, states, chans), F32),
            pltpu.VMEM((total, states, chans), F32),
            pltpu.VMEM((n_tensor, total, chans), BF16),
            pltpu.VMEM((n_expert, 2 * toks, feats // 2), BF16),
            pltpu.VMEM((n_expert, 2 * toks, feats // 2), BF16),
            pltpu.VMEM((toks, feats + LANES), F32),
            pltpu.VMEM((EXP_WIN, CAP, feats + LANES), F32),
            pltpu.VMEM((n_all, CAP, feats + LANES), F32),
            pltpu.VMEM((held, width + LANES), F32),
            pltpu.VMEM((held, expert_gate.shape[1]), BF16),
            pltpu.VMEM((n_expert, CAP, width), F32),
            pltpu.VMEM((n_all, CAP, feats), F32),
            sem((3,)),
            sem((n_all,)),
            sem((n_all,)),
            sem((n_all,)),
            sem((n_all,)),
            sem((n_tensor,)),
            sem((n_tensor,)),
            sem((n_expert,)),
            sem((n_expert,)),
            sem((n_all,)),
            sem((n_all,)),
            sem((n_all,)),
            sem((n_all,)),
        ],
        compiler_params=pltpu.CompilerParams(
            collective_id=0, has_side_effects=True, vmem_limit_bytes=60 * 1024 * 1024
        ),
    )(
        request_lengths,
        expert_ids,
        route_gates,
        mixer_input,
        mixer_gate,
        conv_state,
        conv_weight,
        conv_bias[None],
        ssm_state,
        decay_rate,
        step_bias[None],
        skip_gain[None],
        state_proj,
        step_proj,
        out_proj,
        residual,
        norm_gain[None],
        expert_gate,
        expert_up,
        expert_down,
    )


def solution(mesh):
    in_specs = (
        P("groups", ("expert", "tensor")),
        P("groups", ("expert", "tensor")),
        P("groups", None, ("expert", "tensor")),
        P(None, ("expert", "tensor")),
        P(("expert", "tensor")),
        P("groups", None, ("expert", "tensor")),
        P(None, ("expert", "tensor")),
        P(("expert", "tensor")),
        P(("expert", "tensor")),
        P(("expert", "tensor"), None),
        P(None, ("expert", "tensor")),
        P("expert", "tensor"),
        P(("groups", "expert"), "tensor"),
        P("tensor"),
        P(None, ("expert", "tensor")),
        P(None, ("expert", "tensor")),
        P(("expert", "tensor"), None),
        P(("groups", "expert"), None),
        P(("groups", "expert"), None),
        P("groups"),
    )
    out_specs = (P(("groups", "expert"), "tensor"), P("groups", None, ("expert", "tensor")))
    run = functools.partial(body, mesh.shape["expert"], mesh.shape["tensor"])
    return jax.shard_map(run, mesh=mesh, in_specs=in_specs, out_specs=out_specs, check_vma=False)
```

time: 219 us -> 51.6 us (0.24)
  blocking collectives: 79.1 us -> 0 us
  waiting for transfers between devices: 55.3 us -> 0 us
  Pallas kernels: 0 us -> 42.3 us
  matrix products: 25.3 us -> 0 us
  local copies, waits for them, and re-layouts: 30.3 us -> 8.23 us
  between operations: 14.5 us -> 0.64 us
  starting transfers between devices: 6.8 us -> 0 us
  other arithmetic: 6.36 us -> 0 us
    psum x2 -> x0, blocking collectives: 68.7 us -> none  [the longest x1 63 us: body(): projected = lax.psum(partial_proj, ('expert', 'tensor'))]
    pallas_call x0 -> x1, Pallas kernels: none -> 42.3 us  [body(): pl.pallas_call(functools.partial(kernel, n_expert, n_tensor), out_shape=(...]
    unnamed x3 -> x0, waiting for transfers between devices: 29.8 us -> none
    dot_general x7 -> x0, matrix products: 25.3 us -> none  [the longest x1 12.9 us: body(): jnp.dot(hidden_act, expert_down, preferred_element_type=jnp.float32)]
    reduce_scatter x1 -> x0, waiting for transfers between devices: 15.1 us -> none  [body(): lax.psum_scatter(mixer_part, 'expert', scatter_dimension=0, tiled=True)]
    gather x13 -> x0, local copies, waits for them, and re-layouts: 13.1 us -> none  [the longest x4 5.48 us: convolve(): from_state = conv_state[request, state_slot].astype(jnp.float32)]
    all_gather x2 -> x0, blocking collectives: 10.4 us -> none  [the longest x1 5.25 us: body(): shard_piece = lax.all_gather(arrived, 'tensor', axis=1, tiled=True)]
    all_to_all x2 -> x0, waiting for transfers between devices: 10.4 us -> none  [the longest x1 5.56 us: body(): lax.all_to_all(outgoing, 'expert', split_axis=0, concat_axis=0, tiled=True)]
  transfers between devices with their start and end apart: 4 -> 0, of which waited for: 4 -> 0; matrix products, arithmetic and copies ran while one was open for 1% -> 0% of each run, Pallas kernels for 0% -> 0%
where the time goes in v1:
time: 51.6 us; the launch traced here: 51.2 us
  Pallas kernels  42.3 us (82%)
  local copies, waits for them, and re-layouts  8.23 us (16%)
  between operations  0.64 us (1%)
    pallas_call x1, Pallas kernels, body(): pl.pallas_call(functools.partial(kernel, n_expert, n_tensor), out_shape=(...  42.3 us
    unnamed x6, local copies, waits for them, and re-layouts  8.23 us

profile of v1, /device:TPU:0, one launch (start us, length us, event | category | flops | bytes accessed | tf_op | source)
XLA Modules:
  0.0 51.2 jit_solution(712092099304204220)
XLA Ops:
  0.6 1.3 %copy.22.ids_ref = s32[8,2]{1,0:T(8,128)} copy(s32[8,2]{0,1:T(2,128)} %param.37) | data formatting | bytes 128 | tf_op args[17]
  2.0 1.3 %copy.23.gates_ref = f32[8,2]{1,0:T(8,128)} copy(f32[8,2]{0,1:T(2,128)} %param.38) | data formatting | bytes 128 | tf_op args[18]
  3.3 1.3 %copy.24.conv_state = bf16[8,3,32]{2,1,0:T(4,128)(2,1)} copy(bf16[8,3,32]{2,0,1:T(8,128)(2,1)} %param.22) | data formatting | bytes 3072 | tf_op args[2]
  4.6 1.4 %copy.25.step_proj = bf16[256,32]{1,0:T(8,128)(2,1)} copy(bf16[256,32]{0,1:T(8,128)(2,1)} %param.30) | data formatting | bytes 32768 | tf_op args[10]
  6.1 42.3 %shard_map.203 = (bf16[8,1024]{1,0:T(8,128)(2,1)}, f32[8,16,32]{2,1,0:T(8,128)}) custom-call(s32[8]{0:T(128)} %lengths_ref.1, s32[8,2]{1,0:T(8,128)} %copy.22.ids_ref, f32[8,2]{1,0:T(8,128)} %copy.23.gates_ref, bf16[32,32]{1,0:T(8,128)(2,1)} %mixer_input.1, bf16[32,32]{1,0:T(8,128)(2,1)} %mixer_gate.1, bf16[8,3,32]{2,1,0:T(4,128)(2,1)} %copy.24.conv_state, ...), custom_call_target="tpu_custom_call" | custom-call | tf_op jit(solution)/shard_map/pallas_call | solution.py:421
  48.4 1.3 %copy.28 = bf16[8,1024]{1,0:T(8,128)(2,1)} copy(bf16[8,1024]{1,0:T(8,128)(2,1)} %get-tuple-element.4) | data formatting | bytes 32768
  49.7 1.5 %copy.29 = f32[8,16,32]{2,1,0:T(8,128)} copy(f32[8,16,32]{2,1,0:T(8,128)} %get-tuple-element.5) | data formatting | bytes 32768

commit v2 on v1

--- a/solution.py
+++ b/solution.py
@@ -86,10 +86,10 @@
     my_t = lax.axis_index("tensor")
     me = my_e * n_tensor + my_t
     total, chans = mixer_input.shape
-    requests = conv_state.shape[0]
+    requests = conv_state.shape[1]
     taps = conv_weight.shape[0]
     states = decay_rate.shape[0]
-    rank = step_proj.shape[0]
+    rank = step_proj.shape[1]
     rows_each = total // n_all
     toks, feats = residual.shape
     width = feats * n_tensor
@@ -127,13 +127,13 @@
         ends.append(run)
     place = lax.broadcasted_iota(jnp.int32, (total, chans), 0)
     first = jnp.zeros((total, chans), jnp.int32)
+    old = [conv_state[j].astype(F32) for j in range(taps - 1)]
     from_state = [jnp.zeros((total, chans), F32) for _ in range(taps - 1)]
     for r in range(requests):
         inside = place >= starts[r]
         first = jnp.where(inside, starts[r], first)
-        old = conv_state[r].astype(F32)
         for j in range(taps - 1):
-            from_state[j] = jnp.where(inside, old[j : j + 1, :], from_state[j])
+            from_state[j] = jnp.where(inside, old[j][r : r + 1, :], from_state[j])
     since = place - first
     shifted[0:8, :] = jnp.zeros((8, chans), F32)
     shifted[8:, :] = mixer_input[...].astype(F32)
@@ -200,10 +200,10 @@
         index = [jnp.int32(0) for _ in range(CAP)]
         weight = [jnp.float32(0) for _ in range(CAP)]
         for row in range(toks):
-            zero = ids_ref[row, 0] == w
-            one = ids_ref[row, 1] == w
+            zero = ids_ref[0, row] == w
+            one = ids_ref[1, row] == w
             named = jnp.logical_or(zero, one)
-            gate = jnp.where(zero, gates_ref[row, 0], 0.0) + jnp.where(one, gates_ref[row, 1], 0.0)
+            gate = jnp.where(zero, gates_ref[0, row], 0.0) + jnp.where(one, gates_ref[1, row], 0.0)
             for s in range(CAP):
                 here = jnp.logical_and(named, count == s)
                 index[s] = jnp.where(here, row, index[s])
@@ -218,7 +218,12 @@
     step_low = projected[:, :rank].astype(BF16)
     input_map = projected[:, rank : rank + states]
     output_map = projected[:, rank + states :]
-    raw = jnp.dot(step_low, step_proj[...], preferred_element_type=F32) + step_bias[...]
+    raw = (
+        lax.dot_general(
+            step_low, step_proj[...], (((1,), (1,)), ((), ())), preferred_element_type=F32
+        )
+        + step_bias[...]
+    )
     step = jnp.maximum(raw, 0.0) + jnp.log1p(jnp.exp(-jnp.abs(raw)))
 
     decay_all[...] = jnp.exp(-step[:, None, :] * decay_rate[...][None, :, :])
@@ -380,6 +385,11 @@
         (copy6, n_all),
     ):
         sent_all(copy, count)
+
+
+def finish(layer_in, state_in, layer_out, final_state):
+    layer_out[...] = layer_in[...]
+    final_state[...] = state_in[...]
 
 
 def body(
@@ -418,7 +428,7 @@
     vmem = pl.BlockSpec(memory_space=pltpu.VMEM)
     hbm = pl.BlockSpec(memory_space=pl.ANY)
     sem = pltpu.SemaphoreType.DMA
-    return pl.pallas_call(
+    made = pl.pallas_call(
         functools.partial(kernel, n_expert, n_tensor),
         out_shape=(
             jax.ShapeDtypeStruct((toks, feats), BF16),
@@ -468,11 +478,11 @@
         ),
     )(
         request_lengths,
-        expert_ids,
-        route_gates,
+        expert_ids.T,
+        route_gates.T,
         mixer_input,
         mixer_gate,
-        conv_state,
+        conv_state.transpose(1, 0, 2),
         conv_weight,
         conv_bias[None],
         ssm_state,
@@ -480,7 +490,7 @@
         step_bias[None],
         skip_gain[None],
         state_proj,
-        step_proj,
+        step_proj.T,
         out_proj,
         residual,
         norm_gain[None],
@@ -488,6 +498,12 @@
         expert_up,
         expert_down,
     )
+    return pl.pallas_call(
+        finish,
+        out_shape=tuple(jax.ShapeDtypeStruct(m.shape, m.dtype) for m in made),
+        in_specs=[vmem] * 2,
+        out_specs=(vmem, vmem),
+    )(*made)
 
 
 def solution(mesh):

time: 51.6 us -> 44.7 us (0.87)
  local copies, waits for them, and re-layouts: 8.23 us -> 0 us
  Pallas kernels: 42.3 us -> 43.8 us
    unnamed x6 -> x0, local copies, waits for them, and re-layouts: 8.23 us -> none
    pallas_call x0 -> x1, Pallas kernels: none -> 1.5 us  [body(): pl.pallas_call(finish, out_shape=tuple((jax.ShapeDtypeStruct(m.shape, m.d...]
where the time goes in v2:
time: 44.7 us; the launch traced here: 44.5 us
  Pallas kernels  43.8 us (98%)
  between operations  0.65 us (1%)
    pallas_call x1, Pallas kernels, body(): pl.pallas_call(functools.partial(kernel, n_expert, n_tensor), out_shape=(...  42.3 us
    pallas_call x1, Pallas kernels, body(): pl.pallas_call(finish, out_shape=tuple((jax.ShapeDtypeStruct(m.shape, m.d...  1.5 us

profile of v2, /device:TPU:0, one launch (start us, length us, event | category | flops | bytes accessed | tf_op | source)
XLA Modules:
  0.0 44.5 jit_solution(12102211591156851509)
XLA Ops:
  0.6 42.3 %shard_map.203 = (bf16[8,1024]{1,0:T(8,128)(2,1)}, f32[8,16,32]{2,1,0:T(8,128)}) custom-call(s32[8]{0:T(128)} %lengths_ref.1, s32[2,8]{1,0:T(2,128)} %bitcast.11, f32[2,8]{1,0:T(2,128)} %bitcast.12, bf16[32,32]{1,0:T(8,128)(2,1)} %mixer_input.1, bf16[32,32]{1,0:T(8,128)(2,1)} %mixer_gate.1, bf16[3,8,32]{2,1,0:T(8,128)(2,1)} %bitcast.9, f32[4,32]{1,0:T(4,128)} %conv_weight.1, ...), custom_call_target="tpu_custom_call" | custom-call | tf_op jit(solution)/shard_map/pallas_call | solution.py:431
  43.0 1.5 %shard_map.204 = (bf16[8,1024]{1,0:T(8,128)(2,1)}, f32[8,16,32]{2,1,0:T(8,128)}) custom-call(bf16[8,1024]{1,0:T(8,128)(2,1)} %get-tuple-element.4.layer_in, f32[8,16,32]{2,1,0:T(8,128)} %get-tuple-element.5.state_in), custom_call_target="tpu_custom_call" | custom-call | tf_op jit(solution)/shard_map/pallas_call | solution.py:501

commit v3 on v2

--- a/solution.py
+++ b/solution.py
@@ -62,10 +62,13 @@
     mix_recv,
     stream_s,
     tok_send,
+    tok_held,
     tok_recv,
     tokens_s,
     hidden,
     out_send,
+    out_held,
+    out_part,
     out_recv,
     load_sem,
     s1,
@@ -80,17 +83,21 @@
     r5,
     s6,
     r6,
+    s7,
+    r7,
+    s8,
+    r8,
+    s9,
+    r9,
 ):
-    n_all = n_expert * n_tensor
     my_e = lax.axis_index("expert")
     my_t = lax.axis_index("tensor")
-    me = my_e * n_tensor + my_t
     total, chans = mixer_input.shape
     requests = conv_state.shape[1]
     taps = conv_weight.shape[0]
     states = decay_rate.shape[0]
     rank = step_proj.shape[1]
-    rows_each = total // n_all
+    rows_each = total // n_tensor
     toks, feats = residual.shape
     width = feats * n_tensor
     group = n_expert // EXP_WIN
@@ -103,21 +110,31 @@
     for load in loads:
         load.start()
 
-    def other(k):
-        d = lax.rem(me + k, n_all)
-        return d, d // n_tensor, lax.rem(d, n_tensor)
+    def over_tensor(k):
+        return lax.rem(my_t + k, n_tensor)
+
+    def over_expert(k):
+        return lax.rem(my_e + k, n_expert)
 
     def at(e, t):
         return {"expert": e, "tensor": t}
 
     barrier = pltpu.get_barrier_semaphore()
 
-    def greet(k, _):
-        d, e, t = other(k)
-        pl.semaphore_signal(barrier, inc=1, device_id=at(e, t), device_id_type=MESH)
-        return 0
-
-    lax.fori_loop(1, n_all, greet, 0)
+    def greet_tensor(k, c):
+        pl.semaphore_signal(
+            barrier, inc=1, device_id=at(my_e, over_tensor(k)), device_id_type=MESH
+        )
+        return c
+
+    def greet_expert(k, c):
+        pl.semaphore_signal(
+            barrier, inc=1, device_id=at(over_expert(k), my_t), device_id_type=MESH
+        )
+        return c
+
+    lax.fori_loop(1, n_tensor, greet_tensor, 0)
+    lax.fori_loop(1, n_expert, greet_expert, 0)
 
     starts, ends = [], []
     run = jnp.int32(0)
@@ -151,48 +168,63 @@
     conv_float = conv_out.astype(F32)
 
     partial = jnp.dot(conv_out, state_proj[...], preferred_element_type=F32)
-    for d in range(n_all):
-        part_send[d] = partial[d * rows_each : (d + 1) * rows_each, :]
-    part_recv[me] = part_send[me]
-
-    pl.semaphore_wait(barrier, n_all - 1)
-
-    def copy1(k):
-        d, e, t = other(k)
-        return pltpu.make_async_remote_copy(
-            src_ref=part_send.at[d],
-            dst_ref=part_recv.at[me],
-            send_sem=s1.at[k],
-            recv_sem=r1.at[k],
-            device_id=at(e, t),
-            device_id_type=MESH,
-        )
-
-    def copy2(k):
-        d, e, t = other(k)
-        return pltpu.make_async_remote_copy(
-            src_ref=proj_send,
-            dst_ref=proj_recv.at[me],
-            send_sem=s2.at[k],
-            recv_sem=r2.at[k],
-            device_id=at(e, t),
-            device_id_type=MESH,
-        )
+    for t in range(n_tensor):
+        part_send[t] = partial[t * rows_each : (t + 1) * rows_each, :]
+    part_recv[my_t] = part_send[my_t]
+
+    pl.semaphore_wait(barrier, n_tensor + n_expert - 2)
+
+    def to_tensor(source, target, send, recv):
+        def copy(k):
+            t = over_tensor(k)
+            return pltpu.make_async_remote_copy(
+                src_ref=source(t),
+                dst_ref=target.at[my_t],
+                send_sem=send.at[k],
+                recv_sem=recv.at[k],
+                device_id=at(my_e, t),
+                device_id_type=MESH,
+            )
+
+        return copy
+
+    def to_expert(source, target, send, recv):
+        def copy(k):
+            e = over_expert(k)
+            return pltpu.make_async_remote_copy(
+                src_ref=source(e),
+                dst_ref=target.at[my_e],
+                send_sem=send.at[k],
+                recv_sem=recv.at[k],
+                device_id=at(e, my_t),
+                device_id_type=MESH,
+            )
+
+        return copy
 
     def start_all(copy, count):
-        lax.fori_loop(1, count, lambda k, c: (copy(k).start(), c)[1], 0)
+        for k in range(1, count):
+            copy(k).start()
 
     def receive_all(copy, count):
-        lax.fori_loop(1, count, lambda k, c: (copy(k).wait_recv(), c)[1], 0)
+        for k in range(1, count):
+            copy(k).wait_recv()
 
     def sent_all(copy, count):
-        lax.fori_loop(1, count, lambda k, c: (copy(k).wait_send(), c)[1], 0)
-
-    start_all(copy1, n_all)
-    receive_all(copy1, n_all)
+        for k in range(1, count):
+            copy(k).wait_send()
+
+    copy1 = to_tensor(lambda t: part_send.at[t], part_recv, s1, r1)
+    copy2 = to_expert(lambda e: proj_send, proj_recv, s2, r2)
+    copy7 = to_tensor(lambda t: proj_all.at[my_t], proj_all, s7, r7)
+    start_all(copy1, n_tensor)
+    receive_all(copy1, n_tensor)
     proj_send[...] = jnp.sum(part_recv[...], axis=0)
-    start_all(copy2, n_all)
-    proj_recv[me] = proj_send[...]
+    start_all(copy2, n_expert)
+    proj_recv[my_e] = proj_send[...]
+    receive_all(copy2, n_expert)
+    proj_all[my_t] = jnp.sum(proj_recv[...], axis=0)
+    start_all(copy7, n_tensor)
 
     slots = []
     for w in range(EXP_WIN):
@@ -211,10 +243,8 @@
             count = count + named.astype(jnp.int32)
         slots.append((index, weight))
 
-    receive_all(copy2, n_all)
-    for d in range(n_all):
-        proj_all[d * rows_each : (d + 1) * rows_each, :] = proj_recv[d]
-    projected = proj_all[...]
+    receive_all(copy7, n_tensor)
+    projected = proj_all[...].reshape(total, rank + 2 * states)
     step_low = projected[:, :rank].astype(BF16)
     input_map = projected[:, rank : rank + states]
     output_map = projected[:, rank + states :]
@@ -255,16 +285,7 @@
     mixed = (scanned + skip_gain[...] * conv_float) * silu(mixer_gate[...].astype(F32))
     mixed_all[my_t] = mixed.astype(BF16)
 
-    def copy3(k):
-        return pltpu.make_async_remote_copy(
-            src_ref=mixed_all.at[my_t],
-            dst_ref=mixed_all.at[my_t],
-            send_sem=s3.at[k],
-            recv_sem=r3.at[k],
-            device_id=at(my_e, lax.rem(my_t + k, n_tensor)),
-            device_id_type=MESH,
-        )
-
+    copy3 = to_tensor(lambda t: mixed_all.at[my_t], mixed_all, s3, r3)
     start_all(copy3, n_tensor)
     receive_all(copy3, n_tensor)
     part = jnp.zeros((total, feats), F32)
@@ -278,17 +299,7 @@
         mix_send[e] = jnp.concatenate([rows[:, :half], rows[:, half:]], axis=0).astype(BF16)
     mix_recv[my_e] = mix_send[my_e]
 
-    def copy4(k):
-        e = lax.rem(my_e + k, n_expert)
-        return pltpu.make_async_remote_copy(
-            src_ref=mix_send.at[e],
-            dst_ref=mix_recv.at[my_e],
-            send_sem=s4.at[k],
-            recv_sem=r4.at[k],
-            device_id=at(e, my_t),
-            device_id_type=MESH,
-        )
-
+    copy4 = to_expert(lambda e: mix_send.at[e], mix_recv, s4, r4)
     start_all(copy4, n_expert)
     receive_all(copy4, n_expert)
     mix = jnp.sum(mix_recv[...].astype(F32), axis=0)
@@ -300,31 +311,23 @@
     for w in range(EXP_WIN):
         for s in range(CAP):
             tok_send[w, s : s + 1, :] = stream_s[pl.ds(slots[w][0][s], 1), :]
-    tok_recv[me] = tok_send[my_e // group]
-
-    def copy5(k):
-        d, e, t = other(k)
-        return pltpu.make_async_remote_copy(
-            src_ref=tok_send.at[e // group],
-            dst_ref=tok_recv.at[me],
-            send_sem=s5.at[k],
-            recv_sem=r5.at[k],
-            device_id=at(e, t),
-            device_id_type=MESH,
-        )
-
-    start_all(copy5, n_all)
-    receive_all(copy5, n_all)
+    tok_held[my_e] = tok_send[my_e // group]
+    copy5 = to_expert(lambda e: tok_send.at[e // group], tok_held, s5, r5)
+    start_all(copy5, n_expert)
+    receive_all(copy5, n_expert)
+    for e in range(n_expert):
+        tok_recv[my_t, e * CAP : (e + 1) * CAP, :] = tok_held[e]
+    copy8 = to_tensor(lambda t: tok_recv.at[my_t], tok_recv, s8, r8)
+    start_all(copy8, n_tensor)
+    receive_all(copy8, n_tensor)
     padded = tokens_s.shape[0]
     if padded > held:
         tokens_s[held:, :] = jnp.zeros((padded - held, width + LANES), F32)
-    for e in range(n_expert):
-        square = jnp.zeros((CAP, LANES), F32)
-        for t in range(n_tensor):
-            got = tok_recv[e * n_tensor + t]
-            tokens_s[e * CAP : (e + 1) * CAP, t * feats : (t + 1) * feats] = got[:, :feats]
-            square = square + got[:, feats:]
-        tokens_s[e * CAP : (e + 1) * CAP, width:] = square
+    square = jnp.zeros((held, LANES), F32)
+    for t in range(n_tensor):
+        tokens_s[:held, t * feats : (t + 1) * feats] = tok_recv[t, :, :feats]
+        square = square + tok_recv[t, :, feats:]
+    tokens_s[:held, width:] = square
     scale = lax.rsqrt(tokens_s[:, width : width + 1] / width + EPSILON)
     normed = (tokens_s[:, :width] * scale).astype(BF16)
 
@@ -344,45 +347,52 @@
     loads[2].wait()
     act = hidden[...]
     otile = 512 if feats % 512 == 0 else feats
-
-    def out_tile(i, c):
-        cols = pl.ds(pl.multiple_of(i * otile, otile), otile)
-        got = jnp.dot(act, down_v[:, cols], preferred_element_type=F32)
-        for e in range(n_expert):
-            out_send[e, :, cols] = got[e * CAP : (e + 1) * CAP, :]
+    copy6 = to_tensor(lambda t: out_send.at[t], out_held, s6, r6)
+
+    def out_block(t):
+        def out_tile(i, c):
+            cols = pl.ds(pl.multiple_of(i * otile, otile), otile)
+            base = pl.ds(pl.multiple_of(t * feats + i * otile, otile), otile)
+            got = jnp.dot(act, down_v[:, base], preferred_element_type=F32)
+            out_send[t, :, cols] = got[:held]
+            return c
+
+        lax.fori_loop(0, feats // otile, out_tile, 0)
+
+    def send_block(k, c):
+        out_block(over_tensor(k))
+        copy6(k).start()
         return c
 
-    def copy6(k):
-        d, e, t = other(k)
-        return pltpu.make_async_remote_copy(
-            src_ref=out_send.at[e, :, pl.ds(pl.multiple_of(t * feats, LANES), feats)],
-            dst_ref=out_recv.at[me],
-            send_sem=s6.at[k],
-            recv_sem=r6.at[k],
-            device_id=at(e, t),
-            device_id_type=MESH,
-        )
-
-    lax.fori_loop(0, width // otile, out_tile, 0)
-    start_all(copy6, n_all)
-    out_recv[me] = out_send[my_e, :, pl.ds(pl.multiple_of(my_t * feats, LANES), feats)]
-    receive_all(copy6, n_all)
+    lax.fori_loop(1, n_tensor, send_block, 0)
+    out_block(my_t)
+    out_held[my_t] = out_send[my_t]
+    receive_all(copy6, n_tensor)
+    gathered = jnp.sum(out_held[...], axis=0)
+    for e in range(n_expert):
+        out_part[e] = gathered[e * CAP : (e + 1) * CAP, :]
+    copy9 = to_expert(lambda e: out_part.at[e], out_recv, s9, r9)
+    start_all(copy9, n_expert)
+    out_recv[my_e] = out_part[my_e]
+    receive_all(copy9, n_expert)
     row_id = lax.broadcasted_iota(jnp.int32, (toks, feats), 0)
     result = residual[...].astype(F32) + jnp.concatenate([mix[:toks], mix[toks:]], axis=1)
-    share = group * n_tensor
     for w in range(EXP_WIN):
-        value = jnp.sum(out_recv[w * share : (w + 1) * share], axis=0)
+        value = jnp.sum(out_recv[w * group : (w + 1) * group], axis=0)
         for s in range(CAP):
             index, weight = slots[w]
             result = result + jnp.where(row_id == index[s], weight[s], 0.0) * value[s : s + 1, :]
     layer_out[...] = result.astype(BF16)
     for copy, count in (
-        (copy1, n_all),
-        (copy2, n_all),
+        (copy1, n_tensor),
+        (copy2, n_expert),
+        (copy7, n_tensor),
         (copy3, n_tensor),
         (copy4, n_expert),
-        (copy5, n_all),
-        (copy6, n_all),
+        (copy5, n_expert),
+        (copy8, n_tensor),
+        (copy6, n_tensor),
+        (copy9, n_expert),
     ):
         sent_all(copy, count)
 
@@ -416,13 +426,13 @@
     route_gates,
     request_lengths,
 ):
-    n_all = n_expert * n_tensor
     total, chans = mixer_input.shape
     states = decay_rate.shape[0]
     xw = state_proj.shape[1]
     toks, feats = residual.shape
     width = feats * n_tensor
-    rows_each = total // n_all
+    rows_each = total // n_tensor
+    slots = n_expert * CAP
     held = -(-n_expert * CAP // 16) * 16
     smem = pl.BlockSpec(memory_space=pltpu.SMEM)
     vmem = pl.BlockSpec(memory_space=pltpu.VMEM)
@@ -441,11 +451,11 @@
             pltpu.VMEM(expert_up.shape, BF16),
             pltpu.VMEM(expert_down.shape, BF16),
             pltpu.VMEM((total + 8, chans), F32),
-            pltpu.VMEM((n_all, rows_each, xw), F32),
-            pltpu.VMEM((n_all, rows_each, xw), F32),
+            pltpu.VMEM((n_tensor, rows_each, xw), F32),
+            pltpu.VMEM((n_tensor, rows_each, xw), F32),
             pltpu.VMEM((rows_each, xw), F32),
-            pltpu.VMEM((n_all, rows_each, xw), F32),
-            pltpu.VMEM((total, xw), F32),
+            pltpu.VMEM((n_expert, rows_each, xw), F32),
+            pltpu.VMEM((n_tensor, rows_each, xw), F32),
             pltpu.VMEM((total, states, chans), F32),
             pltpu.VMEM((total, states, chans), F32),
             pltpu.VMEM((total, states, chans), F32),
@@ -454,24 +464,33 @@
             pltpu.VMEM((n_expert, 2 * toks, feats // 2), BF16),
             pltpu.VMEM((toks, feats + LANES), F32),
             pltpu.VMEM((EXP_WIN, CAP, feats + LANES), F32),
-            pltpu.VMEM((n_all, CAP, feats + LANES), F32),
+            pltpu.VMEM((n_expert, CAP, feats + LANES), F32),
+            pltpu.VMEM((n_tensor, slots, feats + LANES), F32),
             pltpu.VMEM((held, width + LANES), F32),
             pltpu.VMEM((held, expert_gate.shape[1]), BF16),
-            pltpu.VMEM((n_expert, CAP, width), F32),
-            pltpu.VMEM((n_all, CAP, feats), F32),
+            pltpu.VMEM((n_tensor, slots, feats), F32),
+            pltpu.VMEM((n_tensor, slots, feats), F32),
+            pltpu.VMEM((n_expert, CAP, feats), F32),
+            pltpu.VMEM((n_expert, CAP, feats), F32),
             sem((3,)),
-            sem((n_all,)),
-            sem((n_all,)),
-            sem((n_all,)),
-            sem((n_all,)),
-            sem((n_tensor,)),
-            sem((n_tensor,)),
-            sem((n_expert,)),
-            sem((n_expert,)),
-            sem((n_all,)),
-            sem((n_all,)),
-            sem((n_all,)),
-            sem((n_all,)),
+            sem((n_tensor,)),
+            sem((n_tensor,)),
+            sem((n_expert,)),
+            sem((n_expert,)),
+            sem((n_tensor,)),
+            sem((n_tensor,)),
+            sem((n_expert,)),
+            sem((n_expert,)),
+            sem((n_expert,)),
+            sem((n_expert,)),
+            sem((n_tensor,)),
+            sem((n_tensor,)),
+            sem((n_tensor,)),
+            sem((n_tensor,)),
+            sem((n_tensor,)),
+            sem((n_tensor,)),
+            sem((n_expert,)),
+            sem((n_expert,)),
         ],
         compiler_params=pltpu.CompilerParams(
             collective_id=0, has_side_effects=True, vmem_limit_bytes=60 * 1024 * 1024

time: 44.7 us -> 47.2 us (1.056)
  Pallas kernels: 43.8 us -> 46.3 us
    pallas_call x1, Pallas kernels: 42.3 us -> 44.8 us  [body(): pl.pallas_call(functools.partial(kernel, n_expert, n_tensor), out_shape=(...]
where the time goes in v3:
time: 47.2 us; the launch traced here: 47 us
  Pallas kernels  46.3 us (98%)
  between operations  0.65 us (1%)
    pallas_call x1, Pallas kernels, body(): pl.pallas_call(functools.partial(kernel, n_expert, n_tensor), out_shape=(...  44.8 us
    pallas_call x1, Pallas kernels, body(): pl.pallas_call(finish, out_shape=tuple((jax.ShapeDtypeStruct(m.shape, m.d...  1.5 us

profile of v3, /device:TPU:0, one launch (start us, length us, event | category | flops | bytes accessed | tf_op | source)
XLA Modules:
  0.0 47.0 jit_solution(2925641645828689433)
XLA Ops:
  0.6 44.8 %shard_map.203 = (bf16[8,1024]{1,0:T(8,128)(2,1)}, f32[8,16,32]{2,1,0:T(8,128)}) custom-call(s32[8]{0:T(128)} %lengths_ref.1, s32[2,8]{1,0:T(2,128)} %bitcast.11, f32[2,8]{1,0:T(2,128)} %bitcast.12, bf16[32,32]{1,0:T(8,128)(2,1)} %mixer_input.1, bf16[32,32]{1,0:T(8,128)(2,1)} %mixer_gate.1, bf16[3,8,32]{2,1,0:T(8,128)(2,1)} %bitcast.9, f32[4,32]{1,0:T(4,128)} %conv_weight.1, ...), custom_call_target="tpu_custom_call" | custom-call | tf_op jit(solution)/shard_map/pallas_call | solution.py:441
  45.5 1.5 %shard_map.204 = (bf16[8,1024]{1,0:T(8,128)(2,1)}, f32[8,16,32]{2,1,0:T(8,128)}) custom-call(bf16[8,1024]{1,0:T(8,128)(2,1)} %get-tuple-element.4.layer_in, f32[8,16,32]{2,1,0:T(8,128)} %get-tuple-element.5.state_in), custom_call_target="tpu_custom_call" | custom-call | tf_op jit(solution)/shard_map/pallas_call | solution.py:520
